TPU v7x, 32 devices: a whole 2x2x4 slice. The times are simulated.
32 devices in a mesh: wide: 8 (over z, y), narrow: 4 (over x, core).
Axes of the slice: x: 2, y: 2, z: 4, core: 2. Of those that a mesh axis runs over, the one named last changes fastest.
Arguments:
- queries: bfloat16 [4096, 2048], P(('wide', 'narrow')), may hold values from -8 to 8
- key_tensor: bfloat16 [4096, 256], P(('wide', 'narrow')), may hold values from -8 to 8
- value_tensor: bfloat16 [4096, 256], P(('wide', 'narrow')), may hold values from -8 to 8
- decay_logarithm: float32 [2, 4096], P(None, ('wide', 'narrow')), may hold values from -2 to 0
- lin_gain: float32 [2048], replicated, may hold values from 0.25 to 1.75
- routes: int32 [4096, 2], P(('wide', 'narrow')), may hold values from 0 to 31, all different within a row; in each aligned block of 128 rows (0 to 127, 128 to 255, ...) at most 12 rows name the same one
- route_weight: float32 [4096, 2], P(('wide', 'narrow')), may hold values from 0.2 to 1
- w_up: bfloat16 [2048, 45056], P(None, 'wide'), may hold values from -0.125 to 0.125
- w_down: bfloat16 [45056, 2048], P('wide'), may hold values from -0.15625 to 0.15625
Outputs:
- layer_out: bfloat16 [4096, 2048], P(('wide', 'narrow'))
Inputs may be any that keep to these rules, and one draw needn't show every extreme that they name: `routes`: each row names 2 different experts. In each aligned block of 128 rows no expert is named more than 12 times, and in some block some expert is named exactly 12 times.
All inputs are finite; a program needn't handle non-finite values.
Results may differ from a plain program's by a relative error of at most 0.0055.
Values may be sent and summed in bfloat16 or wider, within the bound.
A program may use at most 128 MiB of HBM per device.

v0:
```python
import jax
import jax.numpy as jnp
from jax import lax
from jax.sharding import PartitionSpec as P

FF = 1408
EXPERTS = 32
TOP = 2
QUART = 4
WINDOW_KEYS = 128
MOST = 12


def carried_in(x, axis, combine, identity):
    peers, here = (lax.axis_size(axis), lax.axis_index(axis))
    everything = jax.tree.map(lambda part: lax.all_gather(part, axis), x)
    start = jax.tree.map(
        lambda part, zero: jnp.broadcast_to(jnp.asarray(zero, part.dtype), part.shape), x, identity
    )

    def turn(k, before):
        reached = k < here
        new = combine(before, jax.tree.map(lambda part: part[k], everything))
        return jax.tree.map(lambda a, b: jnp.where(reached, a, b), new, before)

    return lax.fori_loop(0, peers, turn, start)


def passed_along(x, axis, by):
    peers = lax.axis_size(axis)
    pairs = [(i, i + by) for i in range(peers) if 0 <= i + by < peers]
    return lax.ppermute(x, axis, pairs)


def chain_step(earlier, later_part):
    decay_early, state_early = earlier
    decay_late, state_late = later_part
    return (decay_early * decay_late, decay_late[:, None, None] * state_early + state_late)


def expert_blocks(received, up_blocks, down_blocks):
    block_count = up_blocks.shape[1]
    feature_width = received.shape[-1]
    token_rows = received.reshape(block_count, -1, feature_width)
    hidden = jnp.einsum("brd,dbh->brh", token_rows, up_blocks, preferred_element_type=jnp.float32)
    hidden = jax.nn.silu(hidden).astype(jnp.bfloat16)
    partial_out = jnp.einsum(
        "brh,bhd->brd", hidden, down_blocks, preferred_element_type=jnp.float32
    )
    return partial_out.astype(jnp.bfloat16).reshape(received.shape)


def per_device(
    queries, key_tensor, value_tensor, decay_logarithm, lin_gain, routes, route_weight, w_up, w_down
):
    tok_count = queries.shape[0]
    model_width = queries.shape[1]
    kv_heads = decay_logarithm.shape[0]
    head_dim = key_tensor.shape[1] // kv_heads
    group_extent = model_width // (kv_heads * head_dim)
    scale_multiplier = head_dim ** (-0.5)
    hi_prec = lax.Precision.HIGHEST
    query_single = queries.astype(jnp.float32).reshape(tok_count, kv_heads, group_extent, head_dim)
    key_single = (
        key_tensor.astype(jnp.float32).reshape(tok_count, kv_heads, head_dim) * scale_multiplier
    )
    value_single = value_tensor.astype(jnp.float32).reshape(tok_count, kv_heads, head_dim)
    cum_decay = jnp.cumsum(decay_logarithm, axis=1)
    end_decay = cum_decay[:, -1]
    position = jnp.arange(tok_count)
    causal = position[:, None] >= position[None, :]
    gap_decay = cum_decay[:, :, None] - cum_decay[:, None, :]
    weight_mask = jnp.where(causal[None], jnp.exp(jnp.where(causal[None], gap_decay, 0.0)), 0.0)
    inner_scores = (
        jnp.einsum("thgd,shd->hgts", query_single, key_single, precision=hi_prec)
        * weight_mask[:, None]
    )
    inner_out = jnp.einsum("hgts,shd->thgd", inner_scores, value_single, precision=hi_prec)
    tail_weight = jnp.exp(end_decay[:, None] - cum_decay)
    local_state = jnp.einsum(
        "shd,she->hde", key_single * tail_weight.T[:, :, None], value_single, precision=hi_prec
    )
    own_part = (jnp.exp(end_decay), local_state)
    identity_part = (
        jnp.ones((kv_heads,), jnp.float32),
        jnp.zeros((kv_heads, head_dim, head_dim), jnp.float32),
    )
    incoming = carried_in(own_part, ("wide", "narrow"), chain_step, identity_part)
    carried = (
        jnp.einsum("thgd,hde->thge", query_single, incoming[1], precision=hi_prec)
        * jnp.exp(cum_decay).T[:, :, None, None]
    )
    linear_heads = (inner_out + carried).reshape(tok_count, -1, head_dim)
    mean_square = jnp.mean(linear_heads * linear_heads, axis=2, keepdims=True)
    normed = (linear_heads / jnp.sqrt(mean_square + 1e-06)).reshape(
        tok_count, model_width
    ) * lin_gain
    prev_keys, prev_values = passed_along((key_tensor, value_tensor), ("wide", "narrow"), 1)
    all_keys = jnp.concatenate([prev_keys, key_tensor], axis=0).reshape(-1, kv_heads, head_dim)
    all_values = jnp.concatenate([prev_values, value_tensor], axis=0).reshape(
        -1, kv_heads, head_dim
    )
    query_bfloat = queries.reshape(tok_count, kv_heads, group_extent, head_dim)
    raw_scores = (
        jnp.einsum("thgd,shd->hgts", query_bfloat, all_keys, preferred_element_type=jnp.float32)
        * scale_multiplier
    )
    key_pos = jnp.arange(WINDOW_KEYS + tok_count) - WINDOW_KEYS
    distance = position[:, None] - key_pos[None, :]
    device_index = lax.axis_index(("wide", "narrow"))
    allowed = (
        (distance >= 0) & (distance < WINDOW_KEYS) & ((key_pos[None, :] >= 0) | (device_index > 0))
    )
    masked = jnp.where(allowed[None, None], raw_scores, -jnp.inf)
    row_max = jnp.max(masked, axis=3, keepdims=True)
    expo_scores = jnp.exp(masked - row_max)
    probs = (expo_scores / jnp.sum(expo_scores, axis=3, keepdims=True)).astype(jnp.bfloat16)
    window_out = jnp.einsum(
        "hgts,shd->thgd", probs, all_values, preferred_element_type=jnp.float32
    ).reshape(tok_count, model_width)
    attn = (normed + window_out).astype(jnp.bfloat16)
    wide_count = lax.axis_size("wide")
    block_units = FF // QUART
    local_blocks = EXPERTS * QUART // wide_count
    up_blocks = w_up.reshape(model_width, local_blocks, block_units)
    down_blocks = w_down.reshape(local_blocks, block_units, model_width)
    flat_routes = routes.reshape(-1)
    onehot = (flat_routes[:, None] == jnp.arange(EXPERTS)[None, :]).astype(jnp.int32)
    earlier_count = jnp.cumsum(onehot, axis=0) - onehot
    slot_rank = jnp.sum(earlier_count * onehot, axis=1).reshape(routes.shape)[:, :, None]
    virtual = routes[:, :, None] * QUART + jnp.arange(QUART)[None, None, :]
    target = virtual // local_blocks
    local_slot = virtual % local_blocks
    total_slots = local_blocks * wide_count * MOST
    slot_index = (local_slot * wide_count + target) * MOST + slot_rank
    layout = (local_blocks, wide_count, MOST, model_width)
    slot_flat = slot_index.reshape(-1)
    token_ids = jnp.broadcast_to(
        jnp.arange(tok_count, dtype=jnp.int32)[:, None, None], slot_index.shape
    ).reshape(-1)
    source_row = jnp.full((total_slots,), tok_count, jnp.int32).at[slot_flat].set(token_ids)
    attn_padded = jnp.concatenate([attn, jnp.zeros((1, model_width), jnp.bfloat16)], axis=0)
    send_rows = attn_padded[source_row].reshape(layout)
    computed = expert_blocks(
        lax.all_to_all(send_rows, "wide", split_axis=1, concat_axis=1, tiled=True),
        up_blocks,
        down_blocks,
    )
    returned = lax.all_to_all(computed, "wide", split_axis=1, concat_axis=1, tiled=True)
    picked = returned.reshape(total_slots, model_width)[slot_flat].reshape(
        tok_count, TOP, QUART, model_width
    )
    block_sum = jnp.sum(picked, axis=2, dtype=jnp.float32)
    moe = jnp.sum(block_sum * route_weight[:, :, None], axis=1)
    return (attn.astype(jnp.float32) + moe).astype(jnp.bfloat16)


def solution(mesh):
    in_specs = (
        P(("wide", "narrow"), None),
        P(("wide", "narrow"), None),
        P(("wide", "narrow"), None),
        P(None, ("wide", "narrow")),
        P(),
        P(("wide", "narrow"), None),
        P(("wide", "narrow"), None),
        P(None, "wide"),
        P("wide", None),
    )
    out_specs = P(("wide", "narrow"), None)
    return jax.shard_map(
        per_device, mesh=mesh, in_specs=in_specs, out_specs=out_specs, check_vma=False
    )
```

profile of v0, /device:TPU:28, one launch (start us, length us, event | category | flops | bytes accessed | tf_op | source)
XLA Modules:
  0.0 521.4 jit_solution(13957870469653140123)
XLA Ops:
  6.5 1.0 reduce_window_sum.26
  8.8 1.7 fusion.34
  10.5 1.9 collective-permute-start
  13.4 3.5 collective-permute-start.1
  19.1 40.4 %all-reduce.1 = f32[64]{0:T(128)S(1)} all-reduce(f32[64]{0:T(128)S(1)} %dynamic-update-slice), channel_id=2, replica_groups=mesh['wide'=8,'narrow'=4] {'wide','narrow'}, use_global_device_ids=true, to_apply=%add.1 | all-reduce | flops 64 | bytes 512
  59.6 1.1 copy.145
  63.7 4.5 scatter_custom_fusion
  68.5 1.4 fusion.7
  70.9 2.2 fusion.57
  73.0 1.9 fusion.18
  74.9 1.3 copy.116
  76.3 33.1 %while.14 = (s32[]{:T(128)}, f32[2,128,128]{2,1,0:T(8,128)S(1)}, s32[]{:T(128)}, f32[32,2]{1,0:T(8,128)S(1)}, f32[32,2,128,128]{3,2,1,0:T(8,128)}, /*index=5*/s32[]{:T(128)}, s32[]{:T(128)}) while((s32[]{:T(128)}, f32[2,128,128]{2,1,0:T(8,128)S(1)}, s32[]{:T(128)}, f32[32,2]{1,0:T(8,128)S(1)}, f32[32,2,128,128]{3,2,1,0:T(8,128)}, ...), condition=%wide.region_2.3_spmd.clone, body=%wide.region_1.2_spmd.clone.sunk | while | flops 131076 | bytes 393345 | solution.py:26
  76.3 1.0 fusion.67
  77.3 1.0 fusion.67
  78.3 1.0 fusion.67
  110.9 1.7 fusion.15
  112.6 7.1 %gather_fusion = bf16[1536,2048]{1,0:T(8,128)(2,1)} fusion(bf16[129,2048]{1,0:T(8,128)(2,1)S(1)} %concatenate.11, s32[2048]{0:T(1024)S(1)} %pad_clamp_fusion), kind=kCustom, calls=%fused_computation | custom fusion | bytes 12589056 | tf_op jit(solution)/shard_map/gather | solution.py:143
  119.7 10.6 %reshape.297 = bf16[16,8,12,2048]{3,2,1,0:T(8,128)(2,1)} reshape(bf16[1536,2048]{1,0:T(8,128)(2,1)} %gather_fusion) | data formatting | bytes 12582912 | tf_op jit(solution)/shard_map/reshape | solution.py:143
  130.3 10.1 %copy.121 = bf16[16,8,12,2048]{3,0,2,1:T(8,128)(2,1)} copy(bf16[16,8,12,2048]{3,2,1,0:T(8,128)(2,1)} %reshape.297) | data formatting | bytes 12582912 | tf_op jit(solution)/shard_map/reshape | solution.py:143
  140.4 6.3 %all-to-all-start = ((bf16[16,8,12,2048]{3,0,2,1:T(8,128)(2,1)}), bf16[16,8,12,2048]{3,0,2,1:T(8,128)(2,1)}, u32[]{:S(2)}, u32[]{:S(2)}) async-start(bf16[16,8,12,2048]{3,0,2,1:T(8,128)(2,1)} %copy.121), calls=%async_computation | async-start | bytes 12582912 | tf_op jit(solution)/shard_map/all_to_all | solution.py:145
  146.7 30.6 %copy.122 = bf16[2048,5632]{0,1:T(8,128)(2,1)} copy(bf16[2048,5632]{1,0:T(8,128)(2,1)} %param.18) | data formatting | bytes 46137344 | tf_op args[7]
  177.3 104.9 %all-to-all-done = bf16[16,8,12,2048]{3,0,2,1:T(8,128)(2,1)} async-done(((bf16[16,8,12,2048]{3,0,2,1:T(8,128)(2,1)}), bf16[16,8,12,2048]{3,0,2,1:T(8,128)(2,1)}, u32[]{:S(2)}, u32[]{:S(2)}) %all-to-all-start) | async-done | bytes 6291488 | tf_op jit(solution)/shard_map/all_to_all | solution.py:145
  282.1 25.6 %convolution_convert_fusion = bf16[16,96,2048]{2,1,0:T(8,128)(2,1)} fusion(bf16[16,352,2048]{2,1,0:T(8,128)(2,1)} %bitcast.122, bf16[2048,16,352]{0,2,1:T(8,128)(2,1)} %bitcast.121, bf16[16,96,2048]{2,0,1:T(8,128)(2,1)} %bitcast.22), kind=kOutput, calls=%fused_computation.9 | convolution fusion | flops 4435034112 | bytes 58720256 | tf_op jit(solution)/shard_map/brh,bhd->brd/dot_general | solution.py:47
  307.7 8.9 %copy.124 = bf16[16,96,2048]{2,0,1:T(8,128)(2,1)} copy(bf16[16,96,2048]{2,1,0:T(8,128)(2,1)} %convolution_convert_fusion) | data formatting | bytes 12582912 | tf_op jit(solution)/shard_map/convert_element_type | solution.py:50
  316.6 7.2 %all-to-all-start.1 = ((bf16[16,8,12,2048]{3,0,2,1:T(8,128)(2,1)}), bf16[16,8,12,2048]{3,0,2,1:T(8,128)(2,1)}, u32[]{:S(2)}, u32[]{:S(2)}) async-start(bf16[16,8,12,2048]{3,0,2,1:T(8,128)(2,1)} %bitcast.123), calls=%async_computation.1 | async-start | bytes 12582912 | tf_op jit(solution)/shard_map/all_to_all | solution.py:149
  324.0 134.8 %all-to-all-done.1 = bf16[16,8,12,2048]{3,0,2,1:T(8,128)(2,1)} async-done(((bf16[16,8,12,2048]{3,0,2,1:T(8,128)(2,1)}), bf16[16,8,12,2048]{3,0,2,1:T(8,128)(2,1)}, u32[]{:S(2)}, u32[]{:S(2)}) %all-to-all-start.1) | async-done | bytes 6291488 | tf_op jit(solution)/shard_map/all_to_all | solution.py:149
  458.8 9.7 %copy.125 = bf16[16,8,12,2048]{3,2,1,0:T(8,128)(2,1)} copy(bf16[16,8,12,2048]{3,0,2,1:T(8,128)(2,1)} %all-to-all-done.1) | data formatting | bytes 12582912 | tf_op jit(solution)/shard_map/all_to_all | solution.py:149
  468.5 10.7 %reshape.302 = bf16[1536,2048]{1,0:T(8,128)(2,1)} reshape(bf16[16,8,12,2048]{3,2,1,0:T(8,128)(2,1)} %copy.125) | data formatting | bytes 12582912 | tf_op jit(solution)/shard_map/reshape | solution.py:150
  479.2 12.4 %gather_fusion.1 = bf16[1024,2048]{1,0:T(8,128)(2,1)} fusion(bf16[1536,2048]{1,0:T(8,128)(2,1)} %reshape.302, s32[1024]{0:T(1024)S(1)} %broadcast_clamp_fusion), kind=kCustom, calls=%fused_computation.1 | custom fusion | bytes 8392704 | tf_op jit(solution)/shard_map/gather | solution.py:150
  491.6 8.5 %reshape.305 = f32[128,2,4,2048]{3,2,1,0:T(4,128)} reshape(bf16[1024,2048]{1,0:T(8,128)(2,1)} %gather_fusion.1) | data formatting | bytes 12582912 | tf_op jit(solution)/shard_map/convert_element_type | solution.py:153
  500.1 9.9 %reduce_sum.48 = f32[128,2,2048]{2,1,0:T(2,128)S(1)} reduce(f32[128,2,4,2048]{3,2,1,0:T(4,128)} %reshape.305, f32[]{:T(128)} %constant.84.clone.1), dimensions={2}, to_apply=%region_10.11 | reduce | flops 1572864 | bytes 10485764 | tf_op jit(solution)/shard_map/reduce_sum | solution.py:153
  510.0 3.2 multiply_reduce_fusion
  (120 shorter events, 40.2 us)
Async XLA Ops:
  6.5 64.2 %copy-start = (bf16[128,256]{1,0:T(8,128)(2,1)S(1)}, bf16[128,256]{1,0:T(8,128)(2,1)}, u32[]{:S(2)}) copy-start(bf16[128,256]{1,0:T(8,128)(2,1)} %param.13) | copy-start | bytes 196612
  6.5 69.7 %all-gather.4.cloned.1.call-start = ((), (), s32[]{:S(2)}) async-start(), calls=%async_computation.2 | async-start | bytes 4325376 | tf_op jit(solution)/shard_map/all_gather | solution.py:16
  10.5 60.2 %collective-permute-start = (bf16[128,256]{1,0:T(8,128)(2,1)}, bf16[128,256]{1,0:T(8,128)(2,1)S(1)}, u32[]{:S(2)}, u32[]{:S(2)}) collective-permute-start(bf16[128,256]{1,0:T(8,128)(2,1)} %param.13), channel_id=1, source_target_pairs={{0,1},{1,2},{2,3},{3,4},{4,5},{5,6},{6,7},{7,8},{8,9},{9,10},{10,1... | collective-permute-start | bytes 196616 | tf_op jit(solution)/shard_map/ppermute | solution.py:32
  13.4 57.4 %collective-permute-start.1 = (bf16[128,256]{0,1:T(8,128)(2,1)S(1)}, bf16[128,256]{0,1:T(8,128)(2,1)S(1)}, u32[]{:S(2)}, u32[]{:S(2)}) collective-permute-start(bf16[128,256]{0,1:T(8,128)(2,1)S(1)} %copy.111), channel_id=1, source_target_pairs={{0,1},{1,2},{2,3},{3,4},{4,5},{5,6},{6,7},{7,8},{8,9},{9,10},{10,1... | collective-permute-start | bytes 196616 | tf_op jit(solution)/shard_map/ppermute | solution.py:32
  76.3 34.6 %copy-start.1 = (f32[2048]{0:T(1024)S(1)}, f32[2048]{0:T(1024)}, u32[]{:S(2)}) copy-start(f32[2048]{0:T(1024)} %param.15) | copy-start | bytes 24580
  140.4 141.7 %all-to-all-start = ((bf16[16,8,12,2048]{3,0,2,1:T(8,128)(2,1)}), bf16[16,8,12,2048]{3,0,2,1:T(8,128)(2,1)}, u32[]{:S(2)}, u32[]{:S(2)}) async-start(bf16[16,8,12,2048]{3,0,2,1:T(8,128)(2,1)} %copy.121), calls=%async_computation | async-start | bytes 12582912 | tf_op jit(solution)/shard_map/all_to_all | solution.py:145
  316.6 7.2 %copy-start.2 = (f32[128,2]{0,1:T(2,128)S(1)}, f32[128,2]{0,1:T(2,128)}, u32[]{:S(2)}) copy-start(f32[128,2]{0,1:T(2,128)} %param.17) | copy-start | bytes 3076
  316.6 142.2 %all-to-all-start.1 = ((bf16[16,8,12,2048]{3,0,2,1:T(8,128)(2,1)}), bf16[16,8,12,2048]{3,0,2,1:T(8,128)(2,1)}, u32[]{:S(2)}, u32[]{:S(2)}) async-start(bf16[16,8,12,2048]{3,0,2,1:T(8,128)(2,1)} %bitcast.123), calls=%async_computation.1 | async-start | bytes 12582912 | tf_op jit(solution)/shard_map/all_to_all | solution.py:149
Sparse Core Ops, SparseCore 0:
  10.6 61.5 all-gather.3
where the time goes:
time: 532 us; the launch traced here: 521 us
  waiting for transfers between devices  240 us (45%)
  local copies, waits for them, and re-layouts  122 us (23%)
  other arithmetic  50.5 us (9%)
  blocking collectives  40.4 us (8%)
  matrix products  34.2 us (6%)
  starting transfers between devices  18.9 us (4%)
  between operations  14.2 us (3%)
    all_to_all x1, waiting for transfers between devices, per_device(): lax.all_to_all(computed, 'wide', split_axis=1, concat_axis=1, tiled=True)  135 us
    all_to_all x1, waiting for transfers between devices, per_device(): lax.all_to_all(send_rows, 'wide', split_axis=1, concat_axis=1, tiled=True)  105 us
    unnamed x1, blocking collectives  40.4 us
    unnamed x13, local copies, waits for them, and re-layouts  33.9 us
    select_n x32, other arithmetic, turn(): return jax.tree.map(lambda a, b: jnp.where(reached, a, b), new, before)  31.8 us
    dot_general x1, matrix products, expert_blocks(): jnp.einsum('brh,bhd->brd', hidden, down_blocks, preferred_element_type=jn...  25.6 us
    reshape x2, local copies, waits for them, and re-layouts, per_device(): send_rows = attn_padded[source_row].reshape(layout)  20.7 us
    gather x1, local copies, waits for them, and re-layouts, per_device(): returned.reshape(total_slots, model_width)[slot_flat]  12.4 us
  transfers between devices with their start and end apart: 5, of which 2 were waited for; matrix products, arithmetic and copies ran while one was open for 10% of the time, Pallas kernels for 0%

commit v1 on v0

v1 whole, which is shorter than its diff:
```python
import functools

import jax
import jax.numpy as jnp
import numpy as np
from jax import lax
from jax.experimental import pallas as pl
from jax.experimental.pallas import tpu as pltpu
from jax.sharding import PartitionSpec as P

FF = 1408
EXPERTS = 32
TOP = 2
QUART = 4
WINDOW_KEYS = 128
MOST = 12
MESH = pl.DeviceIdType.MESH


def dot32(a, b):
    return jnp.dot(a, b, preferred_element_type=jnp.float32)


def slot_tables(wide_count, local_experts, blocks_each, rows):
    expert = np.full((wide_count, rows), -1, np.int32)
    rank = np.full((wide_count, rows), -1, np.int32)
    for d in range(wide_count):
        for e in range(local_experts):
            block = (d * local_experts + e) * blocks_each
            expert[d, e * MOST : (e + 1) * MOST] = block // QUART
            rank[d, e * MOST : (e + 1) * MOST] = np.arange(MOST)
    return expert.reshape(-1), rank.reshape(-1)


def expert_order(wide_count, local_experts, rows):
    order = np.zeros((local_experts, wide_count * MOST, wide_count * rows), np.float32)
    for e in range(local_experts):
        for d in range(wide_count):
            for m in range(MOST):
                order[e, d * MOST + m, d * rows + e * MOST + m] = 1
    return order


def moe_kernel(wide_count, local_experts, chunk, *refs):
    (
        attn_ref, routes_ref, routes_t_ref, gate_ref, slot_row_ref, slot_col_ref, order_ref, back_ref,
        up_hbm, down_hbm, out_ref,
        up, down, pick, send, recv, result, back, returned, gates_hi, gates_lo,
        up_sem, down_sem, send_sem, recv_sem, send_sem2, recv_sem2,
    ) = refs
    me = lax.axis_index("wide")
    hidden_width = up.shape[2]
    tok_count, width = attn_ref.shape
    rows = send.shape[1]
    slots = wide_count * rows

    def up_copy(e):
        cols = slice(e * hidden_width, (e + 1) * hidden_width)
        src = up_hbm if local_experts == 1 else up_hbm.at[:, cols]
        return pltpu.make_async_copy(src, up.at[e], up_sem.at[e])

    def down_copy(e):
        src = down_hbm.at[e * hidden_width : (e + 1) * hidden_width, :]
        return pltpu.make_async_copy(src, down.at[e], down_sem.at[e])

    barrier = pltpu.get_barrier_semaphore()

    @pl.loop(1, wide_count)
    def _(k):
        peer = lax.rem(me + k, wide_count)
        pl.semaphore_signal(barrier, inc=1, device_id={"wide": peer}, device_id_type=MESH)

    before = (
        lax.broadcasted_iota(jnp.int32, (tok_count, tok_count), 0)
        < lax.broadcasted_iota(jnp.int32, (tok_count, tok_count), 1)
    ).astype(jnp.bfloat16)
    after = (
        lax.broadcasted_iota(jnp.int32, (tok_count, tok_count), 0)
        > lax.broadcasted_iota(jnp.int32, (tok_count, tok_count), 1)
    ).astype(jnp.bfloat16)
    expert_col = slot_col_ref[:, 0:1]
    rank_col = slot_col_ref[:, 1:2]
    named_t = (routes_t_ref[0:1, :] == expert_col) | (routes_t_ref[1:2, :] == expert_col)
    rank_t = dot32(named_t.astype(jnp.bfloat16), before)
    picked_t = named_t & (rank_t == rank_col.astype(jnp.float32))
    pick[...] = picked_t.astype(jnp.bfloat16).reshape(pick.shape)

    pl.semaphore_wait(barrier, wide_count - 1)

    def outgoing(peer):
        return pltpu.make_async_remote_copy(
            src_ref=send.at[peer], dst_ref=recv.at[me], send_sem=send_sem.at[peer],
            recv_sem=recv_sem.at[me], device_id={"wide": peer}, device_id_type=MESH,
        )

    def incoming(peer):
        return pltpu.make_async_remote_copy(
            src_ref=send.at[peer], dst_ref=recv.at[peer], send_sem=send_sem.at[peer],
            recv_sem=recv_sem.at[peer], device_id={"wide": peer}, device_id_type=MESH,
        )

    @pl.loop(1, wide_count)
    def _(k):
        peer = lax.rem(me + k, wide_count)
        send[peer] = dot32(pick[peer], attn_ref[...]).astype(jnp.bfloat16)
        outgoing(peer).start()

    for e in range(local_experts):
        up_copy(e).start()
    for e in range(local_experts):
        down_copy(e).start()
    recv[me] = dot32(pick[me], attn_ref[...]).astype(jnp.bfloat16)

    expert_row = slot_row_ref[0:1, :]
    rank_row = slot_row_ref[1:2, :]
    first = routes_ref[:, 0:1] == expert_row
    second = routes_ref[:, 1:2] == expert_row
    rank = dot32(after, (first | second).astype(jnp.bfloat16))
    gate = jnp.where(first, gate_ref[:, 0:1], 0.0) + jnp.where(second, gate_ref[:, 1:2], 0.0)
    gate = jnp.where(rank == rank_row.astype(jnp.float32), gate, 0.0)
    high = gate.astype(jnp.bfloat16)
    gates_hi[...] = high
    gates_lo[...] = (gate - high.astype(jnp.float32)).astype(jnp.bfloat16)

    @pl.loop(1, wide_count)
    def _(k):
        peer = lax.rem(me + k, wide_count)
        incoming(peer).wait_recv()

    for e in range(local_experts):
        up_copy(e).wait()
    for e in range(local_experts):
        down_copy(e).wait()
    chunks = result.shape[1] // chunk

    @pl.loop(0, local_experts * chunks)
    def _(step):
        e = step // chunks
        at = pl.ds(pl.multiple_of((step % chunks) * chunk, chunk), chunk)
        everything = recv.reshape(slots, width)
        if local_experts > 1:
            token_rows = dot32(order_ref[e, at, :], everything[...]).astype(jnp.bfloat16)
        else:
            token_rows = everything[at, :]
        hidden = dot32(token_rows, up[e])
        hidden = (hidden * (1.0 / (1.0 + jnp.exp(-hidden)))).astype(jnp.bfloat16)
        result[e, at, :] = dot32(hidden, down[e]).astype(jnp.bfloat16)

    def homeward(peer, mine):
        return pltpu.make_async_remote_copy(
            src_ref=back.at[peer], dst_ref=returned.at[mine], send_sem=send_sem2.at[peer],
            recv_sem=recv_sem2.at[mine], device_id={"wide": peer}, device_id_type=MESH,
        )

    def rows_for(peer):
        flat = result.reshape(result.shape[0] * result.shape[1], width)
        if local_experts > 1:
            return dot32(back_ref[peer], flat[...]).astype(jnp.bfloat16)
        return flat[pl.ds(pl.multiple_of(peer * rows, rows), rows), :]

    @pl.loop(1, wide_count)
    def _(k):
        peer = lax.rem(me + k, wide_count)
        back[peer] = rows_for(peer)
        homeward(peer, me).start()

    returned[me] = rows_for(me)

    @pl.loop(1, wide_count)
    def _(k):
        peer = lax.rem(me + k, wide_count)
        homeward(peer, peer).wait_recv()

    columns = 512

    @pl.loop(0, width // columns)
    def _(c):
        at = pl.ds(pl.multiple_of(c * columns, columns), columns)
        block = returned.reshape(slots, width)[:, at]
        moe = dot32(gates_hi[...], block) + dot32(gates_lo[...], block)
        out_ref[:, at] = (attn_ref[:, at].astype(jnp.float32) + moe).astype(jnp.bfloat16)

    @pl.loop(1, wide_count)
    def _(k):
        peer = lax.rem(me + k, wide_count)
        outgoing(peer).wait_send()
        homeward(peer, me).wait_send()


def moe_layer(attn, routes, route_weight, w_up, w_down):
    wide_count = lax.axis_size("wide")
    tok_count, width = attn.shape
    units = w_up.shape[1]
    hidden_width = min(units, FF)
    local_experts = units // hidden_width
    blocks_each = hidden_width * QUART // FF
    rows = -(-local_experts * MOST // 16) * 16
    slots = wide_count * rows
    expert, rank = slot_tables(wide_count, local_experts, blocks_each, rows)
    slot_row = np.stack([expert, rank])
    if local_experts > 1:
        order = expert_order(wide_count, local_experts, rows)
        result_rows = wide_count * MOST
        flat = order.reshape(local_experts * result_rows, slots)
        order_back = flat.T.reshape(wide_count, rows, local_experts * result_rows)
    else:
        order = np.zeros((1, 16, 128), np.float32)
        order_back = order
        result_rows = slots
    chunk = result_rows if result_rows <= 128 else 128
    bf = jnp.bfloat16
    vmem = pl.BlockSpec(memory_space=pltpu.VMEM)
    hbm = pl.BlockSpec(memory_space=pltpu.HBM)
    dma = pltpu.SemaphoreType.DMA
    return pl.pallas_call(
        functools.partial(moe_kernel, wide_count, local_experts, chunk),
        out_shape=jax.ShapeDtypeStruct((tok_count, width), bf),
        in_specs=[vmem] * 8 + [hbm] * 2,
        out_specs=vmem,
        scratch_shapes=[
            pltpu.VMEM((local_experts, width, hidden_width), bf),
            pltpu.VMEM((local_experts, hidden_width, width), bf),
            pltpu.VMEM((wide_count, rows, tok_count), bf),
            pltpu.VMEM((wide_count, rows, width), bf),
            pltpu.VMEM((wide_count, rows, width), bf),
            pltpu.VMEM((local_experts, result_rows, width), bf),
            pltpu.VMEM((wide_count, rows, width), bf),
            pltpu.VMEM((wide_count, rows, width), bf),
            pltpu.VMEM((tok_count, slots), bf),
            pltpu.VMEM((tok_count, slots), bf),
            dma((local_experts,)),
            dma((local_experts,)),
            dma((wide_count,)),
            dma((wide_count,)),
            dma((wide_count,)),
            dma((wide_count,)),
        ],
        compiler_params=pltpu.CompilerParams(
            collective_id=0, has_side_effects=True, vmem_limit_bytes=60 * 1024 * 1024
        ),
        name="moe",
    )(
        attn, routes, routes.T, route_weight, jnp.asarray(slot_row), jnp.asarray(slot_row.T),
        jnp.asarray(order, bf), jnp.asarray(order_back, bf), w_up, w_down,
    )


def passed_along(x, axis, by):
    peers = lax.axis_size(axis)
    pairs = [(i, i + by) for i in range(peers) if 0 <= i + by < peers]
    return lax.ppermute(x, axis, pairs)


def carried_in(end_decay, local_state):
    axis = ("wide", "narrow")
    peers, here = lax.axis_size(axis), lax.axis_index(axis)
    decays = lax.all_gather(end_decay, axis)
    states = lax.all_gather(local_state, axis)
    k = jnp.arange(peers)
    between = (k[None, :] > k[:, None]) & (k[None, :] < here)
    gap = jnp.sum(jnp.where(between[:, :, None], decays[None], 0.0), axis=1)
    weight = jnp.where((k < here)[:, None], jnp.exp(gap), 0.0)
    return jnp.sum(weight[:, :, None, None] * states, axis=0)


def per_device(
    queries, key_tensor, value_tensor, decay_logarithm, lin_gain, routes, route_weight, w_up, w_down
):
    tok_count = queries.shape[0]
    model_width = queries.shape[1]
    kv_heads = decay_logarithm.shape[0]
    head_dim = key_tensor.shape[1] // kv_heads
    group_extent = model_width // (kv_heads * head_dim)
    scale_multiplier = head_dim ** (-0.5)
    hi_prec = lax.Precision.HIGHEST
    query_single = queries.astype(jnp.float32).reshape(tok_count, kv_heads, group_extent, head_dim)
    key_single = (
        key_tensor.astype(jnp.float32).reshape(tok_count, kv_heads, head_dim) * scale_multiplier
    )
    value_single = value_tensor.astype(jnp.float32).reshape(tok_count, kv_heads, head_dim)
    position = jnp.arange(tok_count)
    causal = position[:, None] >= position[None, :]
    cum_decay = jnp.sum(jnp.where(causal[None], decay_logarithm[:, None, :], 0.0), axis=2)
    end_decay = cum_decay[:, -1]
    gap_decay = cum_decay[:, :, None] - cum_decay[:, None, :]
    weight_mask = jnp.where(causal[None], jnp.exp(jnp.where(causal[None], gap_decay, 0.0)), 0.0)
    inner_scores = (
        jnp.einsum("thgd,shd->hgts", query_single, key_single, precision=hi_prec)
        * weight_mask[:, None]
    )
    inner_out = jnp.einsum("hgts,shd->thgd", inner_scores, value_single, precision=hi_prec)
    tail_weight = jnp.exp(end_decay[:, None] - cum_decay)
    local_state = jnp.einsum(
        "shd,she->hde", key_single * tail_weight.T[:, :, None], value_single, precision=hi_prec
    )
    incoming = carried_in(end_decay, local_state)
    carried = (
        jnp.einsum("thgd,hde->thge", query_single, incoming, precision=hi_prec)
        * jnp.exp(cum_decay).T[:, :, None, None]
    )
    linear_heads = (inner_out + carried).reshape(tok_count, -1, head_dim)
    mean_square = jnp.mean(linear_heads * linear_heads, axis=2, keepdims=True)
    normed = (linear_heads / jnp.sqrt(mean_square + 1e-06)).reshape(
        tok_count, model_width
    ) * lin_gain
    prev_keys, prev_values = passed_along((key_tensor, value_tensor), ("wide", "narrow"), 1)
    all_keys = jnp.concatenate([prev_keys, key_tensor], axis=0).reshape(-1, kv_heads, head_dim)
    all_values = jnp.concatenate([prev_values, value_tensor], axis=0).reshape(
        -1, kv_heads, head_dim
    )
    query_bfloat = queries.reshape(tok_count, kv_heads, group_extent, head_dim)
    raw_scores = (
        jnp.einsum("thgd,shd->hgts", query_bfloat, all_keys, preferred_element_type=jnp.float32)
        * scale_multiplier
    )
    key_pos = jnp.arange(WINDOW_KEYS + tok_count) - WINDOW_KEYS
    distance = position[:, None] - key_pos[None, :]
    device_index = lax.axis_index(("wide", "narrow"))
    allowed = (
        (distance >= 0) & (distance < WINDOW_KEYS) & ((key_pos[None, :] >= 0) | (device_index > 0))
    )
    masked = jnp.where(allowed[None, None], raw_scores, -jnp.inf)
    row_max = jnp.max(masked, axis=3, keepdims=True)
    expo_scores = jnp.exp(masked - row_max)
    probs = (expo_scores / jnp.sum(expo_scores, axis=3, keepdims=True)).astype(jnp.bfloat16)
    window_out = jnp.einsum(
        "hgts,shd->thgd", probs, all_values, preferred_element_type=jnp.float32
    ).reshape(tok_count, model_width)
    attn = (normed + window_out).astype(jnp.bfloat16)
    return moe_layer(attn, routes, route_weight, w_up, w_down)


def solution(mesh):
    in_specs = (
        P(("wide", "narrow"), None),
        P(("wide", "narrow"), None),
        P(("wide", "narrow"), None),
        P(None, ("wide", "narrow")),
        P(),
        P(("wide", "narrow"), None),
        P(("wide", "narrow"), None),
        P(None, "wide"),
        P("wide", None),
    )
    out_specs = P(("wide", "narrow"), None)
    return jax.shard_map(
        per_device, mesh=mesh, in_specs=in_specs, out_specs=out_specs, check_vma=False
    )
```

time: 532 us -> 177 us (0.33); the launches traced: 521 us -> 177 us
  waiting for transfers between devices: 240 us -> 2.6 us
  local copies, waits for them, and re-layouts: 122 us -> 11.7 us
  Pallas kernels: 0 us -> 88.1 us
  other arithmetic: 50.5 us -> 5.22 us
  matrix products: 34.2 us -> 9.89 us
  starting transfers between devices: 18.9 us -> 5.43 us
    all_to_all x2 -> x0, waiting for transfers between devices: 240 us -> none  [the longest x1 135 us: per_device(): lax.all_to_all(computed, 'wide', split_axis=1, concat_axis=1, tiled=True)]
    pallas_call x0 -> x1, Pallas kernels: none -> 88.1 us  [moe_layer(): pl.pallas_call(functools.partial(moe_kernel, wide_count, local_experts, c...]
    select_n x34 -> x1, other arithmetic: 31.8 us -> 0.01 us  [carried_in(): weight = jnp.where((k < here)[:, None], jnp.exp(gap), 0.0)]
    reshape x4 -> x0, local copies, waits for them, and re-layouts: 31.6 us -> none  [the longest x2 20.7 us: per_device(): send_rows = attn_padded[source_row].reshape(layout)]
    unnamed x13 -> x17, local copies, waits for them, and re-layouts: 33.9 us -> 5.71 us
    dot_general x2 -> x1, matrix products: 26.3 us -> 1.73 us  [per_device(): jnp.einsum('thgd,hde->thge', query_single, incoming, precision=hi_prec)]
    gather x2 -> x0, local copies, waits for them, and re-layouts: 19.5 us -> none  [the longest x1 12.4 us: per_device(): returned.reshape(total_slots, model_width)[slot_flat]]
    convert_element_type x2 -> x0, local copies, waits for them, and re-layouts: 17.4 us -> none  [the longest x1 8.89 us: expert_blocks(): return partial_out.astype(jnp.bfloat16).reshape(received.shape)]
  transfers between devices with their start and end apart: 5 -> 3, of which waited for: 2 -> 1; matrix products, arithmetic and copies ran while one was open for 10% -> 8% of each run, Pallas kernels for 0% -> 0%
where the time goes in v1:
time: 177 us
  Pallas kernels  88.1 us (50%)
  blocking collectives  40 us (23%)
  between operations  13.7 us (8%)
  local copies, waits for them, and re-layouts  11.7 us (7%)
  matrix products  9.89 us (6%)
  starting transfers between devices  5.43 us (3%)
  other arithmetic  5.22 us (3%)
  waiting for transfers between devices  2.6 us (1%)
    pallas_call x1, Pallas kernels, moe_layer(): pl.pallas_call(functools.partial(moe_kernel, wide_count, local_experts, c...  88.1 us
    unnamed x1, blocking collectives  40 us
    unnamed x17, local copies, waits for them, and re-layouts  5.71 us
    ppermute x2, starting transfers between devices, passed_along(): return lax.ppermute(x, axis, pairs)  5.43 us
  transfers between devices with their start and end apart: 3, of which 1 were waited for; matrix products, arithmetic and copies ran while one was open for 8% of the time, Pallas kernels for 0%

profile of v1, /device:TPU:28, one launch (start us, length us, event | category | flops | bytes accessed | tf_op | source)
XLA Modules:
  0.0 176.6 jit_solution(18027188699849888534)
XLA Ops:
  6.6 0.8 select_reduce_fusion
  7.4 0.2 slice_reduce_fusion
  7.6 1.0 copy.152
  8.6 1.7 fusion.26
  10.3 1.9 %collective-permute-start = (bf16[128,256]{1,0:T(8,128)(2,1)}, bf16[128,256]{1,0:T(8,128)(2,1)S(1)}, u32[]{:S(2)}, u32[]{:S(2)}) collective-permute-start(bf16[128,256]{1,0:T(8,128)(2,1)} %param.15), channel_id=1, source_target_pairs={{0,1},{1,2},{2,3},{3,4},{4,5},{5,6},{6,7},{7,8},{8,9},{9,10},{10,1... | collective-permute-start | bytes 196616 | tf_op jit(solution)/shard_map/ppermute | solution.py:251
  12.3 1.0 copy.102
  13.2 3.5 %collective-permute-start.1 = (bf16[128,256]{0,1:T(8,128)(2,1)S(1)}, bf16[128,256]{0,1:T(8,128)(2,1)S(1)}, u32[]{:S(2)}, u32[]{:S(2)}) collective-permute-start(bf16[128,256]{0,1:T(8,128)(2,1)S(1)} %copy.102), channel_id=1, source_target_pairs={{0,1},{1,2},{2,3},{3,4},{4,5},{5,6},{6,7},{7,8},{8,9},{9,10},{10,1... | collective-permute-start | bytes 196616 | tf_op jit(solution)/shard_map/ppermute | solution.py:251
  16.7 0.9 reshape.173
  17.6 0.2 dynamic-update-slice
  17.9 40.0 %all-reduce = f32[64]{0:T(128)S(1)} all-reduce(f32[64]{0:T(128)S(1)} %dynamic-update-slice), channel_id=2, replica_groups=mesh['wide'=8,'narrow'=4] {'wide','narrow'}, use_global_device_ids=true, to_apply=%add | all-reduce | flops 64 | bytes 512
  57.9 0.1 reshape.180
  58.0 0.1 exponential_select_fusion
  58.2 0.1 copy.90
  58.3 1.1 copy.127
  59.6 0.1 fusion.29
  59.8 0.6 fusion.4
  60.4 0.7 convolution_bitcast_fusion.1
  61.2 0.7 copy.108.refs_1_
  61.9 0.7 copy.109.refs_3_
  62.6 0.1 copy.101
  62.8 2.2 %fusion.41 = (f32[2,8,128]{2,1,0:T(8,128)S(1)}, f32[2,8,128,256]{2,3,1,0:T(8,128)}) fusion(pred[128,256]{0,1:T(8,128)(4,1)S(1)} %fusion.29, bf16[256,2,128,1]{0,2,3,1:T(8,128)(2,1)S(1)} %bitcast.97, bf16[128,2,8,128]{3,2,1,0:T(8,128)(2,1)S(1)} %bitcast.87), kind=kOutput, calls=%fused_computation.61 | convolution fusion | flops 136315136 | bytes 2793472 | tf_op jit(solution)/shard_map/sub | solution.py:324
  65.0 3.0 %fusion.10 = f32[2,128,8,128]{3,1,2,0:T(8,128)} fusion(bf16[256,2,128,1]{0,2,3,1:T(8,128)(2,1)S(1)} %bitcast.96, f32[2,8,128,256]{2,3,1,0:T(8,128)} %get-tuple-element.8, f32[2,8,128]{2,1,0:T(8,128)S(1)} %get-tuple-element.7), kind=kOutput, calls=%fused_computation.19 | convolution fusion | flops 135266304 | bytes 3284992 | tf_op jit(solution)/shard_map/hgts,shd->thgd/dot_general | solution.py:326
  68.0 1.6 copy.124
  69.5 2.6 %all-gather.4.cloned.1.call-done = f32[64,128,128]{2,1,0:T(8,128)} async-done(((f32[2,128,128]{2,1,0:T(8,128)}), f32[64,128,128]{2,1,0:T(8,128)}) %all-gather.4.cloned.1.call-update) | async-done | bytes 4194320 | tf_op jit(solution)/shard_map/all_gather | solution.py:258
  72.1 2.5 %multiply_reduce_fusion = f32[2,128,128]{2,1,0:T(8,128)S(1)} fusion(f32[32,2,128,128]{3,2,1,0:T(8,128)} %bitcast.91, f32[32,2]{1,0:T(8,128)S(1)} %copy.94), kind=kLoop, calls=%fused_computation.1 | loop fusion | flops 2064384 | bytes 4325632 | tf_op jit(solution)/shard_map/reduce_sum | solution.py:263
  74.7 1.7 multiply_reduce_fusion.1
  76.4 0.1 copy.100
  76.5 1.6 copy.121
  78.1 0.3 div.27
  78.4 1.4 fusion.7.refs_0_
  79.8 88.1 %moe.1 = bf16[128,2048]{1,0:T(8,128)(2,1)} custom-call(bf16[128,2048]{1,0:T(8,128)(2,1)} %fusion.7.refs_0_, s32[128,2]{1,0:T(8,128)} %copy.108.refs_1_, s32[2,128]{1,0:T(2,128)} %bitcast.98, f32[128,2]{1,0:T(8,128)} %copy.109.refs_3_, s32[2,384]{1,0:T(2,128)} %constant.40.clone.refs_4_, s32[384,2]{1,0:T(8,128)} %constant.41.clone.refs_5_, ...), custom_call_target="tpu_custom_call" | custom-call | tf_op jit(solution)/shard_map/moe/pallas_call | solution.py:215
  167.9 1.9 %copy.159 = bf16[128,2048]{1,0:T(8,128)(2,1)} copy(bf16[128,2048]{1,0:T(8,128)(2,1)} %moe.1) | data formatting | bytes 1048576
  (28 shorter events, 0.5 us)
Async XLA Ops:
  6.5 53.2 %copy-start = (bf16[128,256]{1,0:T(8,128)(2,1)S(1)}, bf16[128,256]{1,0:T(8,128)(2,1)}, u32[]{:S(2)}) copy-start(bf16[128,256]{1,0:T(8,128)(2,1)} %param.14) | copy-start | bytes 196612
  6.5 65.6 %all-gather.4.cloned.1.call-start = ((), (), s32[]{:S(2)}) async-start(), calls=%async_computation | async-start | bytes 4325376 | tf_op jit(solution)/shard_map/all_gather | solution.py:258
  10.3 52.3 %collective-permute-start = (bf16[128,256]{1,0:T(8,128)(2,1)}, bf16[128,256]{1,0:T(8,128)(2,1)S(1)}, u32[]{:S(2)}, u32[]{:S(2)}) collective-permute-start(bf16[128,256]{1,0:T(8,128)(2,1)} %param.15), channel_id=1, source_target_pairs={{0,1},{1,2},{2,3},{3,4},{4,5},{5,6},{6,7},{7,8},{8,9},{9,10},{10,1... | collective-permute-start | bytes 196616 | tf_op jit(solution)/shard_map/ppermute | solution.py:251
  13.2 49.5 %collective-permute-start.1 = (bf16[128,256]{0,1:T(8,128)(2,1)S(1)}, bf16[128,256]{0,1:T(8,128)(2,1)S(1)}, u32[]{:S(2)}, u32[]{:S(2)}) collective-permute-start(bf16[128,256]{0,1:T(8,128)(2,1)S(1)} %copy.102), channel_id=1, source_target_pairs={{0,1},{1,2},{2,3},{3,4},{4,5},{5,6},{6,7},{7,8},{8,9},{9,10},{10,1... | collective-permute-start | bytes 196616 | tf_op jit(solution)/shard_map/ppermute | solution.py:251
  59.4 1.7 copy-start.3
  59.4 2.4 %copy-start.4 = (f32[128,2]{0,1:T(2,128)S(1)}, f32[128,2]{0,1:T(2,128)}, u32[]{:S(2)}) copy-start(f32[128,2]{0,1:T(2,128)} %param.19) | copy-start | bytes 3076
  59.5 3.2 %copy-start.1 = (bf16[128,256]{1,0:T(8,128)(2,1)S(1)}, bf16[128,256]{1,0:T(8,128)(2,1)}, u32[]{:S(2)}) copy-start(bf16[128,256]{1,0:T(8,128)(2,1)} %param.15) | copy-start | bytes 196612
  76.4 2.0 %copy-start.2 = (f32[2048]{0:T(1024)S(1)}, f32[2048]{0:T(1024)}, u32[]{:S(2)}) copy-start(f32[2048]{0:T(1024)} %param.17) | copy-start | bytes 24580
Sparse Core Ops, SparseCore 0:
  10.4 61.6 all-gather.3
